TPU v7x, 256 devices: a whole 4x4x8 slice. The times are simulated.
256 devices in a mesh: row: 16 (over z_lo, x, core), col: 16 (over y, z_hi).
Axes of the slice: x: 4, y: 4, z: 8 (z_hi: 4, z_lo: 2; z = z_hi * 2 + z_lo), core: 2. Of those that a mesh axis runs over, the one named last changes fastest.
Arguments:
- tokens: bfloat16 [1024, 8192], P('col', 'row'), may hold values from -6 to 6
- gate_pre: bfloat16 [1024, 28672], P('row', 'col'), may hold values from -10 to 10
- up_pre: bfloat16 [1024, 28672], P('row', 'col'), may hold values from -6 to 6
- grad_out: bfloat16 [1024, 8192], P('col', 'row'), may hold values from -6 to 6
- gate_weight: bfloat16 [8192, 28672], P('row', 'col'), may hold values from -0.0625 to 0.0625
- up_weight: bfloat16 [8192, 28672], P('row', 'col'), may hold values from -0.0625 to 0.0625
- down_weight: bfloat16 [28672, 8192], P('col', 'row'), may hold values from -0.03125 to 0.03125
Outputs:
- grad_tokens: bfloat16 [1024, 8192], P('col', 'row')
- grad_gate: bfloat16 [8192, 28672], P('row', 'col')
- grad_up: bfloat16 [8192, 28672], P('row', 'col')
- grad_down: bfloat16 [28672, 8192], P('col', 'row')
All inputs are finite; a program needn't handle non-finite values.
Results may differ from a plain program's by a relative error of at most 0.005.
Values may be sent and summed in bfloat16 or wider, within the bound.
A program may use at most 128 MiB of HBM per device.

v0:
```python
import jax
import jax.numpy as jnp
from jax import lax
from jax.sharding import PartitionSpec as P


def gate_backward(hidden_grad, gate_pre, up_pre):
    gate_raw = gate_pre.astype(jnp.float32)
    up_raw = up_pre.astype(jnp.float32)
    sigmoid_gate = jax.nn.sigmoid(gate_raw)
    hidden = (gate_raw * sigmoid_gate * up_raw).astype(jnp.bfloat16)
    gate_grad = (
        hidden_grad * up_raw * sigmoid_gate * (1.0 + gate_raw * (1.0 - sigmoid_gate))
    ).astype(jnp.bfloat16)
    up_grad = (hidden_grad * gate_raw * sigmoid_gate).astype(jnp.bfloat16)
    return (hidden, gate_grad, up_grad)


def on_device(tokens, gate_pre, up_pre, grad_out, gate_weight, up_weight, down_weight):
    contract_last = (((1,), (1,)), ((), ()))
    contract_first = (((0,), (0,)), ((), ()))
    token_panel, grad_panel = (
        lax.all_gather(tokens, "col", axis=0, tiled=True),
        lax.all_gather(grad_out, "col", axis=0, tiled=True),
    )
    hidden_grad = lax.psum_scatter(
        lax.dot_general(grad_panel, down_weight, contract_last, preferred_element_type=jnp.float32),
        "row",
        scatter_dimension=0,
        tiled=True,
    )
    own_hidden, own_gate, own_up = gate_backward(hidden_grad, gate_pre, up_pre)
    hidden, gate_grad, up_grad = (
        lax.all_gather(own_hidden, "row", axis=0, tiled=True),
        lax.all_gather(own_gate, "row", axis=0, tiled=True),
        lax.all_gather(own_up, "row", axis=0, tiled=True),
    )
    summed = lax.dot_general(
        gate_grad, gate_weight, contract_last, preferred_element_type=jnp.float32
    )
    grad_tokens = lax.psum_scatter(
        summed
        + lax.dot_general(up_grad, up_weight, contract_last, preferred_element_type=jnp.float32),
        "col",
        scatter_dimension=0,
        tiled=True,
    ).astype(jnp.bfloat16)
    grad_gate = lax.dot_general(
        token_panel, gate_grad, contract_first, preferred_element_type=jnp.float32
    )
    grad_up = lax.dot_general(
        token_panel, up_grad, contract_first, preferred_element_type=jnp.float32
    )
    grad_down = lax.dot_general(
        hidden, grad_panel, contract_first, preferred_element_type=jnp.float32
    )
    return (
        grad_tokens,
        grad_gate.astype(jnp.bfloat16),
        grad_up.astype(jnp.bfloat16),
        grad_down.astype(jnp.bfloat16),
    )


def solution(mesh):
    in_specs = (
        P("col", "row"),
        P("row", "col"),
        P("row", "col"),
        P("col", "row"),
        P("row", "col"),
        P("row", "col"),
        P("col", "row"),
    )
    out_specs = (P("col", "row"), P("row", "col"), P("row", "col"), P("col", "row"))
    return jax.shard_map(
        on_device, mesh=mesh, in_specs=in_specs, out_specs=out_specs, check_vma=False
    )
```

profile of v0, /device:TPU:1, one launch (start us, length us, event | category | flops | bytes accessed | tf_op | source)
XLA Modules:
  0.0 421.2 jit_solution(12704248937543356519)
XLA Ops:
  7.2 0.0 copy-start
  7.2 0.0 all-gather.6.cloned.1.call-start
  7.2 0.7 all-gather.6.cloned.1.call-update
  7.9 0.0 reduce-scatter.3.cloned.1.call-start
  8.0 58.7 %all-gather.6.cloned.1.call-done = bf16[1024,512]{1,0:T(8,128)(2,1)} async-done(((bf16[64,512]{1,0:T(8,128)(2,1)}), bf16[1024,512]{1,0:T(8,128)(2,1)}) %all-gather.6.cloned.1.call-update) | async-done | bytes 1048592 | tf_op jit(solution)/shard_map/all_gather | solution.py:24
  66.6 6.3 %fusion.12 = f32[1024,1792]{1,0:T(8,128)} fusion(bf16[1024,512]{1,0:T(8,128)(2,1)} %all-gather.6.cloned.1.call-done, bf16[1792,512]{1,0:T(8,128)(2,1)S(1)} %copy-done), kind=kOutput, calls=%fused_computation.22 | convolution fusion | flops 1879048192 | bytes 10223616 | tf_op jit(solution)/shard_map/dot_general | solution.py:27
  72.9 0.0 reduce-scatter.3.cloned.1.call-update
  72.9 0.0 all-gather.8.cloned.1.call-start
  73.0 69.9 %reduce-scatter.3.cloned.1.call-done = f32[64,1792]{1,0:T(8,128)} async-done(((f32[1024,1792]{1,0:T(8,128)}), f32[64,1792]{1,0:T(8,128)}) %reduce-scatter.3.cloned.1.call-update) | async-done | bytes 458768 | tf_op jit(solution)/shard_map/reduce_scatter | solution.py:26
  142.9 2.1 fusion.11
  145.0 0.0 all-gather.8.cloned.1.call-update
  145.0 0.0 all-gather.10.cloned.1.call-start
  145.1 0.5 all-gather.10.cloned.1.call-update
  145.6 0.0 all-gather.12.cloned.1.call-start
  145.6 0.5 all-gather.12.cloned.1.call-update
  146.2 0.0 all-gather.14.cloned.1.call-start
  146.2 0.5 all-gather.14.cloned.1.call-update
  146.8 0.0 reduce-scatter.5.cloned.1.call-start
  146.8 40.2 %all-gather.8.cloned.1.call-done = bf16[1024,1792]{1,0:T(8,128)(2,1)} async-done(((bf16[64,1792]{1,0:T(8,128)(2,1)}), bf16[1024,1792]{1,0:T(8,128)(2,1)}) %all-gather.8.cloned.1.call-update) | async-done | bytes 3670032 | tf_op jit(solution)/shard_map/all_gather | solution.py:35
  187.0 6.1 %fusion.13 = f32[1024,512]{1,0:T(8,128)} fusion(bf16[1024,1792]{1,0:T(8,128)(2,1)} %all-gather.8.cloned.1.call-done, bf16[512,1792]{1,0:T(8,128)(2,1)} %param.11), kind=kOutput, calls=%fused_computation.23 | convolution fusion | flops 1879048192 | bytes 7602176 | tf_op jit(solution)/shard_map/dot_general | solution.py:38
  193.2 35.5 %all-gather.10.cloned.1.call-done = bf16[1024,1792]{1,0:T(8,128)(2,1)} async-done(((bf16[64,1792]{1,0:T(8,128)(2,1)}), bf16[1024,1792]{1,0:T(8,128)(2,1)}) %all-gather.10.cloned.1.call-update) | async-done | bytes 3670032 | tf_op jit(solution)/shard_map/all_gather | solution.py:36
  228.7 6.7 %convolution_add_fusion = f32[1024,512]{1,0:T(8,128)} fusion(f32[1024,512]{1,0:T(8,128)} %fusion.13, bf16[1024,1792]{1,0:T(8,128)(2,1)} %all-gather.10.cloned.1.call-done, bf16[512,1792]{1,0:T(8,128)(2,1)} %param.12), kind=kOutput, calls=%fused_computation.5 | convolution fusion | flops 1879572480 | bytes 9699328 | tf_op jit(solution)/shard_map/dot_general | solution.py:43
  235.4 0.0 reduce-scatter.5.cloned.1.call-update
  235.4 47.5 %all-gather.12.cloned.1.call-done = bf16[1024,512]{1,0:T(8,128)(2,1)} async-done(((bf16[64,512]{1,0:T(8,128)(2,1)}), bf16[1024,512]{1,0:T(8,128)(2,1)}) %all-gather.12.cloned.1.call-update) | async-done | bytes 1048592 | tf_op jit(solution)/shard_map/all_gather | solution.py:23
  283.0 5.7 %fusion = bf16[512,1792]{0,1:T(8,128)(2,1)} fusion(bf16[1024,1792]{1,0:T(8,128)(2,1)} %all-gather.8.cloned.1.call-done, bf16[1024,512]{1,0:T(8,128)(2,1)} %all-gather.12.cloned.1.call-done), kind=kOutput, calls=%fused_computation.3 | convolution fusion | flops 1879965696 | bytes 6553600 | tf_op jit(solution)/shard_map/dot_general | solution.py:48
  288.6 3.9 copy.11
  292.5 5.4 %fusion.1 = bf16[512,1792]{0,1:T(8,128)(2,1)} fusion(bf16[1024,1792]{1,0:T(8,128)(2,1)} %all-gather.10.cloned.1.call-done, bf16[1024,512]{1,0:T(8,128)(2,1)S(1)} %copy-done.4), kind=kOutput, calls=%fused_computation.4 | convolution fusion | flops 1879965696 | bytes 6553600 | tf_op jit(solution)/shard_map/dot_general | solution.py:51
  297.9 3.9 copy.12
  301.8 21.1 %all-gather.14.cloned.1.call-done = bf16[1024,1792]{1,0:T(8,128)(2,1)} async-done(((bf16[64,1792]{1,0:T(8,128)(2,1)}), bf16[1024,1792]{1,0:T(8,128)(2,1)}) %all-gather.14.cloned.1.call-update) | async-done | bytes 3670032 | tf_op jit(solution)/shard_map/all_gather | solution.py:34
  322.9 5.4 %convolution_convert_fusion = bf16[1792,512]{1,0:T(8,128)(2,1)} fusion(bf16[1024,1792]{1,0:T(8,128)(2,1)} %all-gather.14.cloned.1.call-done, bf16[1024,512]{1,0:T(8,128)(2,1)S(1)} %copy-done.3), kind=kOutput, calls=%fused_computation | convolution fusion | flops 1879965696 | bytes 6553600 | tf_op jit(solution)/shard_map/dot_general | solution.py:54
  328.2 84.6 %reduce-scatter.5.cloned.1.call-done = f32[64,512]{1,0:T(8,128)} async-done(((f32[1024,512]{1,0:T(8,128)}), f32[64,512]{1,0:T(8,128)}) %reduce-scatter.5.cloned.1.call-update) | async-done | bytes 131088 | tf_op jit(solution)/shard_map/reduce_scatter | solution.py:41
  412.8 1.5 convert_element_type.37
  (9 shorter events, 0.0 us)
Async XLA Ops:
  7.2 59.5 %copy-start = (bf16[1792,512]{1,0:T(8,128)(2,1)S(1)}, bf16[1792,512]{1,0:T(8,128)(2,1)}, u32[]{:S(2)}) copy-start(bf16[1792,512]{1,0:T(8,128)(2,1)} %param.13) | copy-start | bytes 5505028
  7.2 59.5 %all-gather.6.cloned.1.call-start = ((), (), s32[]{:S(2)}) async-start(), calls=%async_computation.2 | async-start | bytes 1114112 | tf_op jit(solution)/shard_map/all_gather | solution.py:24
  7.9 135.0 %reduce-scatter.3.cloned.1.call-start = ((), (), s32[]{:S(2)}) async-start(), calls=%async_computation.3 | async-start | bytes 7798784 | tf_op jit(solution)/shard_map/reduce_scatter | solution.py:26
  72.9 70.0 %copy-start.1 = (bf16[64,1792]{1,0:T(8,128)(2,1)S(1)}, bf16[64,1792]{1,0:T(8,128)(2,1)}, u32[]{:S(2)}) copy-start(bf16[64,1792]{1,0:T(8,128)(2,1)} %param.8) | copy-start | bytes 688132
  72.9 70.0 %copy-start.2 = (bf16[64,1792]{1,0:T(8,128)(2,1)S(1)}, bf16[64,1792]{1,0:T(8,128)(2,1)}, u32[]{:S(2)}) copy-start(bf16[64,1792]{1,0:T(8,128)(2,1)} %param.9) | copy-start | bytes 688132
  72.9 114.1 %all-gather.8.cloned.1.call-start = ((), (), s32[]{:S(2)}) async-start(), calls=%async_computation.4 | async-start | bytes 3899392 | tf_op jit(solution)/shard_map/all_gather | solution.py:35
  145.0 83.7 %all-gather.10.cloned.1.call-start = ((), (), s32[]{:S(2)}) async-start(), calls=%async_computation.5 | async-start | bytes 3899392 | tf_op jit(solution)/shard_map/all_gather | solution.py:36
  145.6 137.4 %all-gather.12.cloned.1.call-start = ((), (), s32[]{:S(2)}) async-start(), calls=%async_computation.7 | async-start | bytes 1114112 | tf_op jit(solution)/shard_map/all_gather | solution.py:23
  146.2 176.7 %all-gather.14.cloned.1.call-start = ((), (), s32[]{:S(2)}) async-start(), calls=%async_computation.8 | async-start | bytes 3899392 | tf_op jit(solution)/shard_map/all_gather | solution.py:34
  146.8 266.1 %reduce-scatter.5.cloned.1.call-start = ((), (), s32[]{:S(2)}) async-start(), calls=%async_computation.6 | async-start | bytes 2228224 | tf_op jit(solution)/shard_map/reduce_scatter | solution.py:41
  288.6 3.9 copy-start.4
  297.9 24.9 %copy-start.3 = (bf16[1024,512]{1,0:T(8,128)(2,1)S(1)}, bf16[1024,512]{1,0:T(8,128)(2,1)}, u32[]{:S(2)}) copy-start(bf16[1024,512]{1,0:T(8,128)(2,1)} %all-gather.6.cloned.1.call-done) | copy-start | bytes 3145732
Sparse Core Ops, SparseCore 0:
  10.4 56.1 all-gather.5
  73.1 69.7 reduce-scatter.2
  145.3 41.6 all-gather.7
  189.3 39.3 all-gather.9
  231.0 51.9 all-gather.11
  284.7 38.1 all-gather.13
  326.4 86.4 reduce-scatter.4
where the time goes:
time: 423 us; the launch traced here: 421 us
  waiting for transfers between devices  360 us (85%)
  matrix products  35.5 us (8%)
  between operations  14.1 us (3%)
  local copies, waits for them, and re-layouts  7.8 us (2%)
    reduce_scatter x1, waiting for transfers between devices, on_device(): lax.psum_scatter(summed + lax.dot_general(up_grad, up_weight, contract_la...  84.6 us
    reduce_scatter x1, waiting for transfers between devices, on_device(): lax.psum_scatter(lax.dot_general(grad_panel, down_weight, contract_last,...  69.9 us
    all_gather x1, waiting for transfers between devices, on_device(): lax.all_gather(grad_out, 'col', axis=0, tiled=True)  58.7 us
    all_gather x1, waiting for transfers between devices, on_device(): lax.all_gather(tokens, 'col', axis=0, tiled=True)  47.5 us
    all_gather x1, waiting for transfers between devices, on_device(): lax.all_gather(own_gate, 'row', axis=0, tiled=True)  40.2 us
    all_gather x1, waiting for transfers between devices, on_device(): lax.all_gather(own_up, 'row', axis=0, tiled=True)  35.5 us
    all_gather x1, waiting for transfers between devices, on_device(): lax.all_gather(own_hidden, 'row', axis=0, tiled=True)  21.1 us
  transfers between devices with their start and end apart: 7, of which 7 were waited for; matrix products, arithmetic and copies ran while one was open for 9% of the time, Pallas kernels for 0%

commit v1 on v0

v1 whole, which is shorter than its diff:
```python
import jax
import jax.numpy as jnp
from jax import lax
from jax.experimental import pallas as pl
from jax.experimental.pallas import tpu as pltpu
from jax.sharding import PartitionSpec as P

MESH = pl.DeviceIdType.MESH
F32 = jnp.float32
BF16 = jnp.bfloat16

NT = (((1,), (1,)), ((), ()))
TN = (((0,), (0,)), ((), ()))

TOK = 1024
FEAT = 512
HID = 1792
HALF = HID // 2
CHUNK = 256
QUART = 64
ORDER = (2, 1, 3, 0)
N_COPY = 128


def dot(a, b, dims):
    return lax.dot_general(a, b, dims, preferred_element_type=F32)


def kernel(
    tok_in, gate_in, up_in, go_in, wg_in, wu_in, wd_in,
    gt_out, gg_out, gu_out, gd_out,
    wg, wu, wd, tok, go, gate, up, hid, ggrad, ugrad, hg,
    keep, sib_send, sib_recv, x_send, x_recv, acc, z_send, z_recv,
    d_send, d_recv, d_sum, h_send, h_recv,
    send_sem, recv_sem, local_sem,
):
    row = lax.axis_index("row")
    col = lax.axis_index("col")
    zl, x, k = row // 8, (row // 2) % 4, row % 2
    y, zh = col // 4, col % 4
    chip = zl * 4 + x

    def dev(dzl=0, dx=0, dk=0, dy=0, dzh=0):
        return (
            ((zl + dzl) % 2) * 8 + ((x + dx) % 4) * 2 + (k + dk) % 2,
            ((y + dy) % 4) * 4 + (zh + dzh) % 4,
        )

    copies = []

    def send(src, dst, **offset):
        i = len(copies)
        cp = pltpu.make_async_remote_copy(
            src_ref=src, dst_ref=dst, send_sem=send_sem.at[i], recv_sem=recv_sem.at[i],
            device_id=dev(**offset), device_id_type=MESH,
        )
        cp.start()
        copies.append(cp)
        return cp

    locals_ = []

    def load(src, dst):
        cp = pltpu.make_async_copy(src, dst, local_sem.at[len(locals_)])
        cp.start()
        locals_.append(cp)
        return cp

    l_go = load(go_in, go.at[y, zh])
    l_gate = load(gate_in, gate.at[chip, k])
    l_up = load(up_in, up.at[chip, k])
    l_wd = load(wd_in, wd)
    l_tok = load(tok_in, tok.at[y, zh])
    l_wg = load(wg_in, wg)
    l_wu = load(wu_in, wu)

    peers = (
        [dict(dk=1), dict(dzl=1)]
        + [dict(dx=d) for d in (1, 2, 3)]
        + [dict(dy=d) for d in (1, 2, 3)]
        + [dict(dzh=d) for d in (1, 2, 3)]
    )
    barrier = pltpu.get_barrier_semaphore()
    for p in peers:
        pl.semaphore_signal(barrier, inc=1, device_id=dev(**p), device_id_type=MESH)
    pl.semaphore_wait(barrier, len(peers))

    c_go_h = [send(go_in, go.at[y, zh], dzh=d) for d in (1, 2, 3)]
    c_g_x = [send(gate_in, gate.at[chip, k], dx=d) for d in (1, 2, 3)]
    c_u_z = send(up_in, up.at[chip, k], dzl=1)
    c_u_x = [send(up_in, up.at[chip, k], dx=d) for d in (1, 2, 3)]
    c_g_z = [send(gate_in, gate.at[chip, k], dzl=1)]
    c_tok_h = [send(tok_in, tok.at[y, zh], dzh=d) for d in (1, 2, 3)]

    l_go.wait()
    for c in c_go_h:
        c.wait_recv()
    c_go_y = {d: send(go.at[y], go.at[y], dy=d) for d in (2, 1, 3)}

    other = (1 - zl) * 4 + x
    c_u_z.wait_recv()
    c_u_x2 = [send(up.at[other, k], up.at[other, k], dx=d) for d in (1, 2, 3)]

    l_tok.wait()
    for c in c_tok_h:
        c.wait_recv()
    c_tok_y = {d: send(tok.at[y], tok.at[y], dy=d) for d in (2, 1, 3)}

    for d, c in zip((1, 2, 3), c_g_x):
        c.wait_recv()
        at = zl * 4 + (x + 4 - d) % 4
        c_g_z.append(send(gate.at[at, k], gate.at[at, k], dzl=1))

    l_wd.wait()
    mine = pl.ds(pl.multiple_of(k * HALF, 128), HALF)
    theirs = pl.ds(pl.multiple_of((1 - k) * HALF, 128), HALF)
    own = pl.ds(pl.multiple_of(x * QUART, QUART), QUART)
    st = [dict() for _ in ORDER]

    def plane(j):
        return (y + ORDER[j]) % 4

    def s0(j):
        if ORDER[j]:
            c_go_y[4 - ORDER[j]].wait_recv()
        a = go[plane(j)].reshape(CHUNK, FEAT)
        sib_send[j] = dot(a, wd[theirs, :], NT)
        st[j]["sib"] = send(sib_send.at[j], sib_recv.at[j], dk=1)
        keep[j] = dot(a, wd[mine, :], NT)

    def s1(j):
        st[j]["sib"].wait_recv()

        @pl.loop(0, CHUNK // 16)
        def _(i):
            r = pl.ds(pl.multiple_of(i * 16, 16), 16)
            x_send[j, r] = (keep[j, r] + sib_recv[j, r]).astype(BF16)

        st[j]["x"] = []
        for d in (2, 1, 3):
            r = pl.ds(pl.multiple_of((x + d) % 4 * QUART, QUART), QUART)
            st[j]["x"].append(send(x_send.at[j, r], x_recv.at[j, d - 1], dx=d))

    def s2(j):
        for c in st[j]["x"]:
            c.wait_recv()

        @pl.loop(0, QUART // 16)
        def _(i):
            r = pl.ds(pl.multiple_of(i * 16, 16), 16)
            o = pl.ds(pl.multiple_of(x * QUART + i * 16, 16), 16)
            t = keep[j, o] + sib_recv[j, o]
            for d in range(3):
                t = t + x_recv[j, d, r].astype(F32)
            acc[j, r] = t
            z_send[j, r] = t.astype(BF16)

        st[j]["z"] = send(z_send.at[j], z_recv.at[j], dzl=1)

    def s3(j):
        st[j]["z"].wait_recv()
        p = plane(j)

        @pl.loop(0, QUART // 16)
        def _(i):
            r = pl.ds(pl.multiple_of(i * 16, 16), 16)
            o = pl.ds(pl.multiple_of(x * QUART + i * 16, 16), 16)
            hg[k, p, o] = (acc[j, r] + z_recv[j, r].astype(F32)).astype(BF16)

        q = hg.at[k, p, own]
        st[j]["ag"] = [send(q, q, dx=d) for d in (2, 1, 3)]

    def s4(j):
        for c in st[j]["ag"]:
            c.wait_recv()
        q = hg.at[k, plane(j)]
        st[j]["sag"] = send(q, q, dk=1)

    def s5(j):
        st[j]["sag"].wait_recv()
        p = plane(j)
        for b in range(4):
            ch, kk = 2 * p + b // 2, b % 2

            @pl.loop(0, 8)
            def _(i):
                r = pl.ds(pl.multiple_of(i // 2 * 16, 16), 16)
                o = pl.ds(pl.multiple_of(b * 64 + i // 2 * 16, 16), 16)
                h = i % 2
                c = pl.ds(pl.multiple_of(h * HALF, 128), HALF)
                g = gate[ch, kk, r, c].astype(F32)
                u = up[ch, kk, r, c].astype(F32)
                t = hg[h, p, o].astype(F32)
                s = 1.0 / (1.0 + jnp.exp(-g))
                ts = t * s
                ggrad[p, o, c] = (ts * u * (1.0 + g * (1.0 - s))).astype(BF16)
                ugrad[p, o, c] = (ts * g).astype(BF16)

        part = dot(ggrad[p], wg[...], NT) + dot(ugrad[p], wu[...], NT)
        if ORDER[j]:
            d_send[ORDER[j] - 1] = part
            st[j]["d"] = send(d_send.at[ORDER[j] - 1], d_recv.at[ORDER[j] - 1], dy=ORDER[j])
        else:
            d_sum[...] = part

    s0(0)
    s0(1)
    s1(0)
    s0(2)
    s1(1)
    s0(3)
    s1(2)
    s1(3)

    for c in c_g_z:
        c.wait_recv()
    for c in c_u_x + c_u_x2:
        c.wait_recv()
    l_gate.wait()
    l_up.wait()
    c_g_s = send(gate.at[:, k], gate.at[:, k], dk=1)
    c_u_s = send(up.at[:, k], up.at[:, k], dk=1)

    s2(0)
    s3(0)
    s2(1)
    s3(1)

    c_g_s.wait_recv()
    c_u_s.wait_recv()

    @pl.loop(0, 64)
    def _(i):
        r = pl.ds(pl.multiple_of(i % 4 * 16, 16), 16)
        b = i // 4
        o = pl.ds(pl.multiple_of(b % 4 * 64 + i % 4 * 16, 16), 16)
        g = gate[b // 2, b % 2, r].astype(F32)
        u = up[b // 2, b % 2, r].astype(F32)
        hid[b // 4, o] = (g * u * (1.0 / (1.0 + jnp.exp(-g)))).astype(BF16)

    l_wg.wait()
    l_wu.wait()
    s4(0)
    s2(2)
    s3(2)
    s5(0)
    s4(1)
    s2(3)
    s3(3)
    s5(1)

    def grad_down():
        b = go[...].reshape(TOK, FEAT)

        @pl.loop(0, 7)
        def _(i):
            c = pl.ds(pl.multiple_of(i * 256, 256), 256)
            a = hid[:, :, c].reshape(TOK, 256)
            gd_out[c, :] = dot(a, b, TN).astype(BF16)

    grad_down()
    s4(2)
    s5(2)
    s4(3)
    s5(3)

    for j in range(3):
        st[j]["d"].wait_recv()
    tot = d_sum[...] + d_recv[0] + d_recv[1] + d_recv[2]
    d_sum[...] = tot
    h_send[...] = tot.astype(BF16)
    c_h = []
    for d in (2, 1, 3):
        r = pl.ds(pl.multiple_of((zh + d) % 4 * 64, 64), 64)
        c_h.append(send(h_send.at[r], h_recv.at[d - 1], dzh=d))

    for d in (1, 2, 3):
        c_tok_y[d].wait_recv()
    a = tok[...].reshape(TOK, FEAT)

    @pl.loop(0, 7)
    def _(i):
        c = pl.ds(pl.multiple_of(i * 256, 256), 256)
        gg_out[:, c] = dot(a, ggrad[:, :, c].reshape(TOK, 256), TN).astype(BF16)
        gu_out[:, c] = dot(a, ugrad[:, :, c].reshape(TOK, 256), TN).astype(BF16)

    for c in c_h:
        c.wait_recv()
    t = d_sum[pl.ds(pl.multiple_of(zh * 64, 64), 64), :]
    for d in range(3):
        t = t + h_recv[d].astype(F32)
    gt_out[...] = t.astype(BF16)
    for c in copies:
        c.wait_send()


def on_device(tokens, gate_pre, up_pre, grad_out, gate_weight, up_weight, down_weight):
    hbm = pl.BlockSpec(memory_space=pl.ANY)
    vmem = pl.BlockSpec(memory_space=pltpu.VMEM)
    bf = lambda *s: pltpu.VMEM(s, BF16)
    fl = lambda *s: pltpu.VMEM(s, F32)
    return pl.pallas_call(
        kernel,
        out_shape=(
            jax.ShapeDtypeStruct((64, FEAT), BF16),
            jax.ShapeDtypeStruct((FEAT, HID), BF16),
            jax.ShapeDtypeStruct((FEAT, HID), BF16),
            jax.ShapeDtypeStruct((HID, FEAT), BF16),
        ),
        in_specs=[hbm] * 7,
        out_specs=(vmem,) * 4,
        scratch_shapes=[
            bf(FEAT, HID), bf(FEAT, HID), bf(HID, FEAT),
            bf(4, 4, 64, FEAT), bf(4, 4, 64, FEAT),
            bf(8, 2, 64, HID), bf(8, 2, 64, HID),
            bf(4, CHUNK, HID), bf(4, CHUNK, HID), bf(4, CHUNK, HID),
            bf(2, 4, CHUNK, HALF),
            fl(4, CHUNK, HALF), fl(4, CHUNK, HALF), fl(4, CHUNK, HALF),
            bf(4, CHUNK, HALF), bf(4, 3, QUART, HALF),
            fl(4, QUART, HALF), bf(4, QUART, HALF), bf(4, QUART, HALF),
            fl(3, CHUNK, FEAT), fl(3, CHUNK, FEAT), fl(CHUNK, FEAT),
            bf(CHUNK, FEAT), bf(3, 64, FEAT),
            pltpu.SemaphoreType.DMA((N_COPY,)),
            pltpu.SemaphoreType.DMA((N_COPY,)),
            pltpu.SemaphoreType.DMA((8,)),
        ],
        compiler_params=pltpu.CompilerParams(
            collective_id=0, has_side_effects=True, vmem_limit_bytes=62 * 2**20
        ),
        cost_estimate=pl.CostEstimate(
            flops=12 * TOK * FEAT * HID, bytes_accessed=2**24, transcendentals=TOK * HID
        ),
        name="swiglu_backward",
    )(tokens, gate_pre, up_pre, grad_out, gate_weight, up_weight, down_weight)


def solution(mesh):
    in_specs = (
        P("col", "row"),
        P("row", "col"),
        P("row", "col"),
        P("col", "row"),
        P("row", "col"),
        P("row", "col"),
        P("col", "row"),
    )
    out_specs = (P("col", "row"), P("row", "col"), P("row", "col"), P("col", "row"))
    return jax.shard_map(
        on_device, mesh=mesh, in_specs=in_specs, out_specs=out_specs, check_vma=False
    )
```

time: 423 us -> 124 us (0.29)
  waiting for transfers between devices: 360 us -> 0 us
  Pallas kernels: 0 us -> 115 us
  matrix products: 35.5 us -> 0 us
  between operations: 14.1 us -> 0.64 us
    all_gather x5 -> x0, waiting for transfers between devices: 203 us -> none  [the longest x1 58.7 us: on_device(): lax.all_gather(grad_out, 'col', axis=0, tiled=True)]
    reduce_scatter x2 -> x0, waiting for transfers between devices: 155 us -> none  [the longest x1 84.6 us: on_device(): lax.psum_scatter(summed + lax.dot_general(up_grad, up_weight, contract_la...]
    pallas_call x0 -> x1, Pallas kernels: none -> 115 us  [on_device(): pl.pallas_call(kernel, out_shape=(jax.ShapeDtypeStruct((64, FEAT), BF16),...]
    dot_general x6 -> x0, matrix products: 35.5 us -> none  [the longest x1 6.74 us: on_device(): lax.dot_general(up_grad, up_weight, contract_last, preferred_element_type...]
  transfers between devices with their start and end apart: 7 -> 0, of which waited for: 7 -> 0; matrix products, arithmetic and copies ran while one was open for 9% -> 0% of each run, Pallas kernels for 0% -> 0%
where the time goes in v1:
time: 124 us
  Pallas kernels  115 us (93%)
  local copies, waits for them, and re-layouts  7.85 us (6%)
    pallas_call x1, Pallas kernels, on_device(): pl.pallas_call(kernel, out_shape=(jax.ShapeDtypeStruct((64, FEAT), BF16),...  115 us
    unnamed x8, local copies, waits for them, and re-layouts  7.85 us

profile of v1, /device:TPU:1, one launch (start us, length us, event | category | flops | bytes accessed | tf_op | source)
XLA Modules:
  0.0 123.7 jit_solution(1374286027388112096)
XLA Ops:
  0.6 115.2 %swiglu_backward.1 = (bf16[64,512]{1,0:T(8,128)(2,1)}, bf16[512,1792]{1,0:T(8,128)(2,1)}, bf16[512,1792]{1,0:T(8,128)(2,1)}, bf16[1792,512]{1,0:T(8,128)(2,1)}) custom-call(bf16[64,512]{1,0:T(8,128)(2,1)} %tok_in.1, bf16[64,1792]{1,0:T(8,128)(2,1)} %gate_in.1, bf16[64,1792]{1,0:T(8,128)(2,1)} %up_in.1, bf16[64,512]{1,0:T(8,128)(2,1)} %go_in.1, ...), custom_call_target="tpu_custom_call" | custom-call | flops 11274289152 | bytes 16777216 | tf_op jit(solution)/shard_map/swiglu_backward/pallas_call | solution.py:302
  115.9 1.5 %copy.15 = bf16[64,512]{1,0:T(8,128)(2,1)} copy(bf16[64,512]{1,0:T(8,128)(2,1)} %get-tuple-element.8) | data formatting | bytes 131072
  117.4 0.0 copy-start.1
  117.4 3.0 %copy.16 = bf16[512,1792]{1,0:T(8,128)(2,1)} copy(bf16[512,1792]{1,0:T(8,128)(2,1)} %get-tuple-element.9) | data formatting | bytes 3670016
  120.3 0.0 copy-done.1
  120.3 0.0 copy-start
  120.3 1.2 copy.17
  121.6 0.9 copy-done
  122.5 1.2 copy.18
Async XLA Ops:
  117.4 3.0 %copy-start.1 = (bf16[512,1792]{1,0:T(8,128)(2,1)S(1)}, bf16[512,1792]{1,0:T(8,128)(2,1)}, u32[]{:S(2)}) copy-start(bf16[512,1792]{1,0:T(8,128)(2,1)} %get-tuple-element.10) | copy-start | bytes 5505028
  120.3 2.2 %copy-start = (bf16[1792,512]{1,0:T(8,128)(2,1)S(1)}, bf16[1792,512]{1,0:T(8,128)(2,1)}, u32[]{:S(2)}) copy-start(bf16[1792,512]{1,0:T(8,128)(2,1)} %get-tuple-element.11) | copy-start | bytes 5505028

commit v2 on v1

v2 whole, which is shorter than its diff:
```python
import jax
import jax.numpy as jnp
from jax import lax
from jax.experimental import pallas as pl
from jax.experimental.pallas import tpu as pltpu
from jax.sharding import PartitionSpec as P

MESH = pl.DeviceIdType.MESH
F32 = jnp.float32
BF16 = jnp.bfloat16

NN = (((1,), (0,)), ((), ()))
TN = (((0,), (0,)), ((), ()))

TOK = 1024
FEAT = 512
HID = 1792
HALF = HID // 2
PLANE = 256
CHUNK = 128
PART = 32
ORDER = ((2, 1), (2, 0), (3, 1), (0, 1), (1, 1), (1, 0), (3, 0), (0, 0))
N_COPY = 192
SCHEDULE = (
    ("turn_down",), ("turn_up",), ("go_y",), ("gate_relay",), ("s0", 3), ("s0", 7), ("up_relay",),
    ("s1", 3), ("s1", 7), ("gate_last",), ("up_other",), ("s0", 0), ("s0", 1), ("s2", 3), ("s1", 0),
    ("s1", 1), ("tok_h",), ("s2", 7), ("s0", 2), ("s0", 4), ("s0", 5), ("s0", 6), ("s1", 2),
    ("s1", 4), ("s1", 5), ("up_other_relay",), ("s1", 6), ("s2", 0), ("s2", 1), ("s2", 2),
    ("s2", 4), ("s3", 3), ("s2", 5), ("gather_core",), ("s2", 6), ("s3", 7), ("tok_y",), ("s3", 0),
    ("s5", 3), ("s3", 1), ("s3", 2), ("core_arrive",), ("hidden",), ("s6", 3), ("s5", 0), ("s3", 4),
    ("grad_down",), ("s5", 1), ("s6", 0), ("s3", 5), ("s6", 1), ("s5", 2), ("s5", 7), ("s3", 6),
    ("s6", 2), ("s5", 4), ("s6", 7), ("s6", 4), ("s5", 5), ("s6", 5), ("s5", 6), ("s6", 6),
    ("s7", 1), ("wg",), ("s7", 0), ("final",),
)


def dot(a, b, dims):
    return lax.dot_general(a, b, dims, preferred_element_type=F32)


def ds(start, size):
    return pl.ds(pl.multiple_of(start, size), size)


def kernel(
    tok_in, gate_in, up_in, go_in, wg_in, wu_in, wd_in,
    gt_out, gg_out, gu_out, gd_out,
    wg, wu, wd, wg_t, wu_t, wd_t, tok, go, gate, up, hid, ggrad, ugrad, hg,
    keep, sib_send, sib_recv, x_send, x_recv, acc, z_send, z_recv,
    d_send, d_recv, d_sum, h_send, h_recv,
    send_sem, recv_sem, local_sem,
):
    row = lax.axis_index("row")
    col = lax.axis_index("col")
    zl, x, k = row // 8, (row // 2) % 4, row % 2
    y, zh = col // 4, col % 4
    chip = zl * 4 + x

    def dev(dzl=0, dx=0, dk=0, dy=0, dzh=0):
        return (
            ((zl + dzl) % 2) * 8 + ((x + dx) % 4) * 2 + (k + dk) % 2,
            ((y + dy) % 4) * 4 + (zh + dzh) % 4,
        )

    copies = []

    def prepare(src, dst, **offset):
        i = len(copies)
        cp = pltpu.make_async_remote_copy(
            src_ref=src, dst_ref=dst, send_sem=send_sem.at[i], recv_sem=recv_sem.at[i],
            device_id=dev(**offset), device_id_type=MESH,
        )
        copies.append(cp)
        return cp

    def send(src, dst, **offset):
        cp = prepare(src, dst, **offset)
        cp.start()
        return cp

    def arrive(group):
        for c in group:
            c.wait_recv()

    def both_ways(q):
        return send(q, q, dx=1), send(q, q, dx=3)

    def relay(pair, q_left, q_right, rows):
        pair[0].wait_recv()
        q = q_left(slice(0, rows // 2))
        to_right = send(q, q, dx=1)
        pair[1].wait_recv()
        q = q_right(slice(rows // 2, rows))
        return to_right, send(q, q, dx=3)

    locals_ = []

    def load(src, dst):
        cp = pltpu.make_async_copy(src, dst, local_sem.at[len(locals_)])
        cp.start()
        locals_.append(cp)
        return cp

    l_go = load(go_in, go.at[y, zh])
    l_wd = load(wd_in, wd)
    l_gate = load(gate_in, gate.at[chip, k])
    l_up = load(up_in, up.at[chip, k])
    l_tok = load(tok_in, tok.at[y, zh])
    l_wg = load(wg_in, wg)
    l_wu = load(wu_in, wu)

    peers = (
        [dict(dk=1), dict(dzl=1)]
        + [dict(dx=d) for d in (1, 2, 3)]
        + [dict(dy=d) for d in (1, 2, 3)]
        + [dict(dzh=d) for d in (1, 2, 3)]
    )
    barrier = pltpu.get_barrier_semaphore()
    for p in peers:
        pl.semaphore_signal(barrier, inc=1, device_id=dev(**p), device_id_type=MESH)
    pl.semaphore_wait(barrier, len(peers))

    other = (1 - zl) * 4 + x
    left, right, across = (zl * 4 + (x + d) % 4 for d in (3, 1, 2))
    o_left, o_right = ((1 - zl) * 4 + (x + d) % 4 for d in (3, 1))
    mine = ds(k * HALF, HALF)
    theirs = ds((1 - k) * HALF, HALF)
    st = [dict() for _ in ORDER]
    got = {}
    planes = set()

    def plane(j):
        return (y + ORDER[j][0]) % 4

    def rows(j, start, size):
        return ds(ORDER[j][1] * CHUNK + start, size)

    def s0(j):
        dy, half = ORDER[j]
        if dy and dy not in planes:
            planes.add(dy)
            got["go_y"][4 - dy].wait_recv()
        a = go[plane(j), 2 * half : 2 * half + 2].reshape(CHUNK, FEAT)
        sib_send[j] = dot(a, wd_t[:, theirs], NN)
        st[j]["sib"] = send(sib_send.at[j], sib_recv.at[j], dk=1)
        keep[j] = dot(a, wd_t[:, mine], NN)

    def s1(j):
        st[j]["sib"].wait_recv()

        @pl.loop(0, CHUNK // 16)
        def _(i):
            r = ds(i * 16, 16)
            x_send[j, r] = (keep[j, r] + sib_recv[j, r]).astype(BF16)

        st[j]["x"] = []
        for d in (2, 1, 3):
            r = ds((x + d) % 4 * PART, PART)
            st[j]["x"].append(send(x_send.at[j, r], x_recv.at[j, d - 1], dx=d))

    def s2(j):
        arrive(st[j]["x"])
        for i in range(PART // 16):
            r = pl.ds(i * 16, 16)
            o = ds(x * PART + i * 16, 16)
            t = keep[j, o] + sib_recv[j, o]
            for d in range(3):
                t = t + x_recv[j, d, r].astype(F32)
            acc[j, r] = t
            z_send[j, r] = t.astype(BF16)
        st[j]["z"] = send(z_send.at[j], z_recv.at[j], dzl=1)

    def s3(j):
        st[j]["z"].wait_recv()
        p = plane(j)
        for i in range(PART // 16):
            r = pl.ds(i * 16, 16)
            hg[k, p, rows(j, x * PART + i * 16, 16)] = (
                acc[j, r] + z_recv[j, r].astype(F32)
            ).astype(BF16)
        q = hg.at[k, p, rows(j, x * PART, PART)]
        st[j]["ar"] = [send(q, q, dx=d) for d in (2, 1, 3)]

    def s5(j):
        arrive(st[j]["ar"])
        q = hg.at[k, plane(j), rows(j, 0, CHUNK)]
        st[j]["core"] = send(q, q, dk=1)

    def s6(j):
        st[j]["core"].wait_recv()
        p = plane(j)
        dy, half = ORDER[j]
        for b in range(2):

            @pl.loop(0, 8, unroll=4)
            def _(i):
                r = ds(i // 2 * 16, 16)
                o = rows(j, b * 64 + i // 2 * 16, 16)
                h = i % 2
                c = ds(h * HALF, HALF)
                g = gate[2 * p + half, b, r, c].astype(F32)
                u = up[2 * p + half, b, r, c].astype(F32)
                t = hg[h, p, o].astype(F32)
                s = 1.0 / (1.0 + jnp.exp(-g))
                ts = t * s
                ggrad[p, o, c] = (ts * u * (1.0 + g * (1.0 - s))).astype(BF16)
                ugrad[p, o, c] = (ts * g).astype(BF16)

        o = rows(j, 0, CHUNK)
        part = dot(ggrad[p, o], wg_t[...], NN) + dot(ugrad[p, o], wu_t[...], NN)
        if dy:
            d_send[dy - 1, o] = part.astype(BF16)
            st[j]["d"] = send(d_send.at[dy - 1, o], d_recv.at[dy - 1, o], dy=dy)
        else:
            d_sum[o] = part

    def s7(half):
        for j, (dy, h) in enumerate(ORDER):
            if dy and h == half:
                st[j]["d"].wait_recv()
        o = pl.ds(half * CHUNK, CHUNK)
        t = d_sum[o]
        for d in range(3):
            t = t + d_recv[d, o].astype(F32)
        d_sum[o] = t
        h_send[o] = t.astype(BF16)
        for d, c in got["h"].items():

            @pl.when((zh + d) % 4 // 2 == half)
            def _():
                c.start()

    def hidden():
        @pl.loop(0, 64, unroll=4)
        def _(i):
            r = ds(i % 4 * 16, 16)
            b = i // 4
            o = ds(b % 4 * 64 + i % 4 * 16, 16)
            g = gate[b // 2, b % 2, r].astype(F32)
            u = up[b // 2, b % 2, r].astype(F32)
            hid[b // 4, o] = (g * u * (1.0 / (1.0 + jnp.exp(-g)))).astype(BF16)

    def grad_down():
        a, b = hid[...].reshape(TOK, HID), go[...].reshape(TOK, FEAT)
        gd_out[...] = dot(a, b, TN).astype(BF16)

    def tok_h():
        got["tok_h"] = [send(tok_in, tok.at[y, zh], dzh=d) for d in (2, 1, 3)]

    def tok_y():
        l_tok.wait()
        arrive(got["tok_h"])
        got["tok_y"] = [send(tok.at[y], tok.at[y], dy=d) for d in (2, 1, 3)]

    def gate_z(at):
        got["g_z"].append(send(gate.at[at, k], gate.at[at, k], dzl=1))

    def gate_relay():
        got["g_r"] = relay(
            got["g_x"], lambda r: gate.at[left, k, r], lambda r: gate.at[right, k, r], 64
        )
        gate_z(left)
        gate_z(right)

    def gate_last():
        arrive(got["g_r"])
        gate_z(across)

    def up_relay():
        got["u_r"] = relay(
            got["u_x"], lambda r: up.at[left, k, r], lambda r: up.at[right, k, r], 64
        )

    def up_other():
        got["u_z"].wait_recv()
        got["u_x2"] = both_ways(up.at[other, k])

    def up_other_relay():
        got["u_r2"] = relay(
            got["u_x2"], lambda r: up.at[o_left, k, r], lambda r: up.at[o_right, k, r], 64
        )

    def gather_core():
        arrive(got["g_z"])
        arrive(got["u_r"])
        arrive(got["u_r2"])
        l_gate.wait()
        l_up.wait()
        got["core"] = [
            send(gate.at[:, k], gate.at[:, k], dk=1),
            send(up.at[:, k], up.at[:, k], dk=1),
        ]

    got["h"] = {
        d: prepare(h_send.at[ds((zh + d) % 4 * 64, 64)], h_recv.at[d - 1], dzh=d)
        for d in (2, 1, 3)
    }

    def go_y():
        arrive(go_h)
        l_go.wait()
        got["go_y"] = {d: send(go.at[y], go.at[y], dy=d) for d in (2, 1, 3)}
        got["u_z"] = send(up_in, up.at[chip, k], dzl=1)
        got["g_z"] = [send(gate_in, gate.at[chip, k], dzl=1)]

    def core_arrive():
        arrive(got["core"])

    def turn_down():
        l_wd.wait()
        wd_t[...] = wd[...].T

    def turn_up():
        l_wg.wait()
        l_wu.wait()
        wg_t[...] = wg[...].T
        wu_t[...] = wu[...].T

    def wg_grads():
        arrive(got["tok_y"])
        a = tok[...].reshape(TOK, FEAT)
        gg_out[...] = dot(a, ggrad[...].reshape(TOK, HID), TN).astype(BF16)
        gu_out[...] = dot(a, ugrad[...].reshape(TOK, HID), TN).astype(BF16)

    def final():
        arrive(got["h"].values())
        t = d_sum[ds(zh * 64, 64), :]
        for d in range(3):
            t = t + h_recv[d].astype(F32)
        gt_out[...] = t.astype(BF16)

    go_h = [send(go_in, go.at[y, zh], dzh=d) for d in (2, 1, 3)]
    q = gate.at[chip, k]
    got["g_x"] = send(gate_in, q, dx=1), send(gate_in, q, dx=3)
    q = up.at[chip, k]
    got["u_x"] = send(up_in, q, dx=1), send(up_in, q, dx=3)

    steps = dict(
        turn_down=turn_down,
        turn_up=turn_up,
        go_y=go_y,
        gate_relay=gate_relay,
        s0=s0,
        up_relay=up_relay,
        s1=s1,
        gate_last=gate_last,
        up_other=up_other,
        s2=s2,
        tok_h=tok_h,
        up_other_relay=up_other_relay,
        s3=s3,
        gather_core=gather_core,
        tok_y=tok_y,
        s5=s5,
        core_arrive=core_arrive,
        hidden=hidden,
        s6=s6,
        grad_down=grad_down,
        s7=s7,
        wg=wg_grads,
        final=final,
    )
    for name, *at in SCHEDULE:
        steps[name](*at)
    for c in copies:
        c.wait_send()


def store(a, b, c, d, a_out, b_out, c_out, d_out, sem):
    moves = [
        pltpu.make_async_copy(src, dst, sem.at[i])
        for i, (src, dst) in enumerate(((b, b_out), (c, c_out), (d, d_out), (a, a_out)))
    ]
    for m in moves:
        m.start()
    for m in moves:
        m.wait()


def on_device(tokens, gate_pre, up_pre, grad_out, gate_weight, up_weight, down_weight):
    hbm = pl.BlockSpec(memory_space=pl.ANY)
    vmem = pl.BlockSpec(memory_space=pltpu.VMEM)
    bf = lambda *s: pltpu.VMEM(s, BF16)
    fl = lambda *s: pltpu.VMEM(s, F32)
    n = len(ORDER)
    made = pl.pallas_call(
        kernel,
        out_shape=(bf(64, FEAT), bf(FEAT, HID), bf(FEAT, HID), bf(HID, FEAT)),
        in_specs=[hbm] * 7,
        out_specs=(vmem,) * 4,
        scratch_shapes=[
            bf(FEAT, HID), bf(FEAT, HID), bf(HID, FEAT),
            bf(HID, FEAT), bf(HID, FEAT), bf(FEAT, HID),
            bf(4, 4, 64, FEAT), bf(4, 4, 64, FEAT),
            bf(8, 2, 64, HID), bf(8, 2, 64, HID),
            bf(4, PLANE, HID), bf(4, PLANE, HID), bf(4, PLANE, HID),
            bf(2, 4, PLANE, HALF),
            fl(n, CHUNK, HALF), fl(n, CHUNK, HALF), fl(n, CHUNK, HALF),
            bf(n, CHUNK, HALF), bf(n, 3, PART, HALF),
            fl(n, PART, HALF), bf(n, PART, HALF), bf(n, PART, HALF),
            bf(3, PLANE, FEAT), bf(3, PLANE, FEAT), fl(PLANE, FEAT),
            bf(PLANE, FEAT), bf(3, 64, FEAT),
            pltpu.SemaphoreType.DMA((N_COPY,)),
            pltpu.SemaphoreType.DMA((N_COPY,)),
            pltpu.SemaphoreType.DMA((8,)),
        ],
        compiler_params=pltpu.CompilerParams(
            collective_id=0, has_side_effects=True, vmem_limit_bytes=57 * 2**20
        ),
        cost_estimate=pl.CostEstimate(
            flops=12 * TOK * FEAT * HID, bytes_accessed=2**24, transcendentals=TOK * HID
        ),
        name="swiglu_backward",
    )(tokens, gate_pre, up_pre, grad_out, gate_weight, up_weight, down_weight)
    return pl.pallas_call(
        store,
        out_shape=tuple(jax.ShapeDtypeStruct(m.shape, BF16) for m in made),
        in_specs=[vmem] * 4,
        out_specs=(hbm,) * 4,
        scratch_shapes=[pltpu.SemaphoreType.DMA((4,))],
        compiler_params=pltpu.CompilerParams(vmem_limit_bytes=2**20),
        name="store",
    )(*(pltpu.with_memory_space_constraint(m, pltpu.VMEM) for m in made))


def solution(mesh):
    in_specs = (
        P("col", "row"),
        P("row", "col"),
        P("row", "col"),
        P("col", "row"),
        P("row", "col"),
        P("row", "col"),
        P("col", "row"),
    )
    out_specs = (P("col", "row"), P("row", "col"), P("row", "col"), P("col", "row"))
    return jax.shard_map(
        on_device, mesh=mesh, in_specs=in_specs, out_specs=out_specs, check_vma=False
    )
```

time: 124 us -> 96.8 us (0.78)
  Pallas kernels: 115 us -> 95.1 us
  local copies, waits for them, and re-layouts: 7.85 us -> 0 us
    pallas_call x1 -> x2, Pallas kernels: 115 us -> 95.1 us  [the longest x1 92.7 us: on_device(): pl.pallas_call(kernel, out_shape=(bf(64, FEAT), bf(FEAT, HID), bf(FEAT, H...]
    unnamed x8 -> x0, local copies, waits for them, and re-layouts: 7.85 us -> none
where the time goes in v2:
time: 96.8 us; the launch traced here: 95.9 us
  Pallas kernels  95.1 us (98%)
    pallas_call x1, Pallas kernels, on_device(): pl.pallas_call(kernel, out_shape=(bf(64, FEAT), bf(FEAT, HID), bf(FEAT, H...  92.7 us
    pallas_call x1, Pallas kernels, on_device(): pl.pallas_call(store, out_shape=tuple((jax.ShapeDtypeStruct(m.shape, BF16...  2.48 us

profile of v2, /device:TPU:1, one launch (start us, length us, event | category | flops | bytes accessed | tf_op | source)
XLA Modules:
  0.0 95.9 jit_solution(16691963091738039799)
XLA Ops:
  0.6 92.7 %swiglu_backward.1 = (bf16[64,512]{1,0:T(8,128)(2,1)S(1)}, bf16[512,1792]{1,0:T(8,128)(2,1)S(1)}, bf16[512,1792]{1,0:T(8,128)(2,1)S(1)}, bf16[1792,512]{1,0:T(8,128)(2,1)S(1)}) custom-call(bf16[64,512]{1,0:T(8,128)(2,1)} %tok_in.1, bf16[64,1792]{1,0:T(8,128)(2,1)} %gate_in.1, bf16[64,1792]{1,0:T(8,128)(2,1)} %up_in.1, bf16[64,512]{1,0:T(8,128)(2,1)} %go_in.1, ...), custom_call_target="tpu_custom_call" | custom-call | flops 11274289152 | bytes 16777216 | tf_op jit(solution)/shard_map/swiglu_backward/pallas_call | solution.py:386
  93.3 2.5 %store.1 = (bf16[64,512]{1,0:T(8,128)(2,1)}, bf16[512,1792]{1,0:T(8,128)(2,1)}, bf16[512,1792]{1,0:T(8,128)(2,1)}, bf16[1792,512]{1,0:T(8,128)(2,1)}) custom-call(bf16[64,512]{1,0:T(8,128)(2,1)S(1)} %get-tuple-element.8.a, bf16[512,1792]{1,0:T(8,128)(2,1)S(1)} %get-tuple-element.9.b, bf16[512,1792]{1,0:T(8,128)(2,1)S(1)} %get-tuple-element.10.c, ...), custom_call_target="tpu_custom_call" | custom-call | tf_op jit(solution)/shard_map/store/pallas_call | solution.py:415

commit v3 on v2

--- a/solution.py
+++ b/solution.py
@@ -19,18 +19,20 @@
 PLANE = 256
 CHUNK = 128
 PART = 32
-ORDER = ((2, 1), (2, 0), (3, 1), (0, 1), (1, 1), (1, 0), (3, 0), (0, 0))
+ORDER = ((1, 0), (0, 0), (2, 1), (3, 0), (3, 1), (1, 1), (0, 1), (2, 0))
+DIRECT = ((1, 0), (0, 0), (2, 1), (3, 0), (3, 1), (1, 1))
 N_COPY = 192
 SCHEDULE = (
-    ("turn_down",), ("turn_up",), ("go_y",), ("gate_relay",), ("s0", 3), ("s0", 7), ("up_relay",),
-    ("s1", 3), ("s1", 7), ("gate_last",), ("up_other",), ("s0", 0), ("s0", 1), ("s2", 3), ("s1", 0),
-    ("s1", 1), ("tok_h",), ("s2", 7), ("s0", 2), ("s0", 4), ("s0", 5), ("s0", 6), ("s1", 2),
-    ("s1", 4), ("s1", 5), ("up_other_relay",), ("s1", 6), ("s2", 0), ("s2", 1), ("s2", 2),
-    ("s2", 4), ("s3", 3), ("s2", 5), ("gather_core",), ("s2", 6), ("s3", 7), ("tok_y",), ("s3", 0),
-    ("s5", 3), ("s3", 1), ("s3", 2), ("core_arrive",), ("hidden",), ("s6", 3), ("s5", 0), ("s3", 4),
-    ("grad_down",), ("s5", 1), ("s6", 0), ("s3", 5), ("s6", 1), ("s5", 2), ("s5", 7), ("s3", 6),
-    ("s6", 2), ("s5", 4), ("s6", 7), ("s6", 4), ("s5", 5), ("s6", 5), ("s5", 6), ("s6", 6),
-    ("s7", 1), ("wg",), ("s7", 0), ("final",),
+    ("g_x",), ("uz",), ("u_x",), ("turn_down",), ("turn_up",), ("gz0",), ("g_relay",), ("gz12",),
+    ("go_y",), ("s0", 1), ("s0", 6), ("u_other",), ("u_relay",), ("s0", 7), ("gz3",), ("s0", 0),
+    ("s0", 4), ("s1", 7), ("s1", 0), ("s0", 3), ("u_other_relay",), ("s0", 5), ("s1", 3), ("s0", 2),
+    ("s1", 5), ("s2", 7), ("s1", 4), ("s2", 0), ("gather_core",), ("tok_h",), ("s3", 7), ("s2", 3),
+    ("s1", 2), ("s3", 0), ("s2", 5), ("s1", 1), ("s2", 4), ("s4", 7), ("s1", 6), ("s2", 2),
+    ("tok_y",), ("s3", 3), ("s5", 0), ("s3", 5), ("core_arrive",), ("hidden",), ("s3", 2),
+    ("s3", 4), ("grad_down",), ("s5", 7), ("s2", 1), ("s2", 6), ("s6", 0), ("s5", 3), ("s6", 7),
+    ("s3", 1), ("s5", 5), ("s3", 6), ("s6", 3), ("s5", 2), ("s6", 5), ("s5", 4), ("s6", 2),
+    ("s5", 1), ("s6", 4), ("s4", 6), ("s6", 1), ("s7", 0), ("s5", 6), ("s6", 6), ("s7", 1), ("wg",),
+    ("final",),
 )
 
 
@@ -102,12 +104,6 @@
         return cp
 
     l_go = load(go_in, go.at[y, zh])
-    l_wd = load(wd_in, wd)
-    l_gate = load(gate_in, gate.at[chip, k])
-    l_up = load(up_in, up.at[chip, k])
-    l_tok = load(tok_in, tok.at[y, zh])
-    l_wg = load(wg_in, wg)
-    l_wu = load(wu_in, wu)
 
     peers = (
         [dict(dk=1), dict(dzl=1)]
@@ -127,7 +123,6 @@
     theirs = ds((1 - k) * HALF, HALF)
     st = [dict() for _ in ORDER]
     got = {}
-    planes = set()
 
     def plane(j):
         return (y + ORDER[j][0]) % 4
@@ -137,9 +132,8 @@
 
     def s0(j):
         dy, half = ORDER[j]
-        if dy and dy not in planes:
-            planes.add(dy)
-            got["go_y"][4 - dy].wait_recv()
+        if dy:
+            got["go_y"][4 - dy, half].wait_recv()
         a = go[plane(j), 2 * half : 2 * half + 2].reshape(CHUNK, FEAT)
         sib_send[j] = dot(a, wd_t[:, theirs], NN)
         st[j]["sib"] = send(sib_send.at[j], sib_recv.at[j], dk=1)
@@ -179,7 +173,18 @@
                 acc[j, r] + z_recv[j, r].astype(F32)
             ).astype(BF16)
         q = hg.at[k, p, rows(j, x * PART, PART)]
-        st[j]["ar"] = [send(q, q, dx=d) for d in (2, 1, 3)]
+        if ORDER[j] in DIRECT:
+            st[j]["ar"] = [send(q, q, dx=d) for d in (2, 1, 3)]
+        else:
+            st[j]["ag"] = both_ways(q)
+
+    def s4(j):
+        p = plane(j)
+
+        def at(pos):
+            return lambda r: hg.at[k, p, rows(j, pos % 4 * PART + r.start, 16)]
+
+        st[j]["ar"] = relay(st[j]["ag"], at(x + 3), at(x + 1), PART)
 
     def s5(j):
         arrive(st[j]["ar"])
@@ -252,30 +257,45 @@
         arrive(got["tok_h"])
         got["tok_y"] = [send(tok.at[y], tok.at[y], dy=d) for d in (2, 1, 3)]
 
-    def gate_z(at):
-        got["g_z"].append(send(gate.at[at, k], gate.at[at, k], dzl=1))
-
-    def gate_relay():
+    def g_x():
+        q = gate.at[chip, k]
+        got["g_x"] = send(gate_in, q, dx=1), send(gate_in, q, dx=3)
+
+    def u_x():
+        q = up.at[chip, k]
+        got["u_x"] = send(up_in, q, dx=1), send(up_in, q, dx=3)
+
+    def uz():
+        got["u_z"] = send(up_in, up.at[chip, k], dzl=1)
+
+    def gate_z(*places):
+        got["g_z"] += [send(gate.at[at, k], gate.at[at, k], dzl=1) for at in places]
+
+    def gz0():
+        got["g_z"].append(send(gate_in, gate.at[chip, k], dzl=1))
+
+    def g_relay():
         got["g_r"] = relay(
             got["g_x"], lambda r: gate.at[left, k, r], lambda r: gate.at[right, k, r], 64
         )
-        gate_z(left)
-        gate_z(right)
-
-    def gate_last():
+
+    def gz12():
+        gate_z(left, right)
+
+    def gz3():
         arrive(got["g_r"])
         gate_z(across)
 
-    def up_relay():
+    def u_relay():
         got["u_r"] = relay(
             got["u_x"], lambda r: up.at[left, k, r], lambda r: up.at[right, k, r], 64
         )
 
-    def up_other():
+    def u_other():
         got["u_z"].wait_recv()
         got["u_x2"] = both_ways(up.at[other, k])
 
-    def up_other_relay():
+    def u_other_relay():
         got["u_r2"] = relay(
             got["u_x2"], lambda r: up.at[o_left, k, r], lambda r: up.at[o_right, k, r], 64
         )
@@ -299,9 +319,10 @@
     def go_y():
         arrive(go_h)
         l_go.wait()
-        got["go_y"] = {d: send(go.at[y], go.at[y], dy=d) for d in (2, 1, 3)}
-        got["u_z"] = send(up_in, up.at[chip, k], dzl=1)
-        got["g_z"] = [send(gate_in, gate.at[chip, k], dzl=1)]
+        got["go_y"] = {}
+        for d, h in ((2, 0), (3, 0), (1, 1), (1, 0), (3, 1), (2, 1)):
+            q = go.at[y, 2 * h : 2 * h + 2]
+            got["go_y"][d, h] = send(q, q, dy=d)
 
     def core_arrive():
         arrive(got["core"])
@@ -330,32 +351,41 @@
         gt_out[...] = t.astype(BF16)
 
     go_h = [send(go_in, go.at[y, zh], dzh=d) for d in (2, 1, 3)]
-    q = gate.at[chip, k]
-    got["g_x"] = send(gate_in, q, dx=1), send(gate_in, q, dx=3)
-    q = up.at[chip, k]
-    got["u_x"] = send(up_in, q, dx=1), send(up_in, q, dx=3)
+    got["g_z"] = []
+    l_wd = load(wd_in, wd)
+    l_gate = load(gate_in, gate.at[chip, k])
+    l_up = load(up_in, up.at[chip, k])
+    l_tok = load(tok_in, tok.at[y, zh])
+    l_wg = load(wg_in, wg)
+    l_wu = load(wu_in, wu)
 
     steps = dict(
+        g_x=g_x,
+        uz=uz,
+        u_x=u_x,
         turn_down=turn_down,
         turn_up=turn_up,
+        gz0=gz0,
+        g_relay=g_relay,
+        gz12=gz12,
         go_y=go_y,
-        gate_relay=gate_relay,
         s0=s0,
-        up_relay=up_relay,
+        u_other=u_other,
+        u_relay=u_relay,
+        gz3=gz3,
         s1=s1,
-        gate_last=gate_last,
-        up_other=up_other,
+        u_other_relay=u_other_relay,
         s2=s2,
+        gather_core=gather_core,
         tok_h=tok_h,
-        up_other_relay=up_other_relay,
         s3=s3,
-        gather_core=gather_core,
+        s4=s4,
         tok_y=tok_y,
         s5=s5,
         core_arrive=core_arrive,
         hidden=hidden,
+        grad_down=grad_down,
         s6=s6,
-        grad_down=grad_down,
         s7=s7,
         wg=wg_grads,
         final=final,

time: 96.8 us -> 91.3 us (0.943)
  Pallas kernels: 95.1 us -> 90.4 us
    pallas_call x1, Pallas kernels: 92.7 us -> 87.9 us  [on_device(): pl.pallas_call(kernel, out_shape=(bf(64, FEAT), bf(FEAT, HID), bf(FEAT, H...]
where the time goes in v3:
time: 91.3 us; the launch traced here: 91.2 us
  Pallas kernels  90.4 us (99%)
    pallas_call x1, Pallas kernels, on_device(): pl.pallas_call(kernel, out_shape=(bf(64, FEAT), bf(FEAT, HID), bf(FEAT, H...  87.9 us
    pallas_call x1, Pallas kernels, on_device(): pl.pallas_call(store, out_shape=tuple((jax.ShapeDtypeStruct(m.shape, BF16...  2.48 us

profile of v3, /device:TPU:1, one launch (start us, length us, event | category | flops | bytes accessed | tf_op | source)
XLA Modules:
  0.0 91.2 jit_solution(3824161534002591867)
XLA Ops:
  0.6 87.9 %swiglu_backward.1 = (bf16[64,512]{1,0:T(8,128)(2,1)S(1)}, bf16[512,1792]{1,0:T(8,128)(2,1)S(1)}, bf16[512,1792]{1,0:T(8,128)(2,1)S(1)}, bf16[1792,512]{1,0:T(8,128)(2,1)S(1)}) custom-call(bf16[64,512]{1,0:T(8,128)(2,1)} %tok_in.1, bf16[64,1792]{1,0:T(8,128)(2,1)} %gate_in.1, bf16[64,1792]{1,0:T(8,128)(2,1)} %up_in.1, bf16[64,512]{1,0:T(8,128)(2,1)} %go_in.1, ...), custom_call_target="tpu_custom_call" | custom-call | flops 11274289152 | bytes 16777216 | tf_op jit(solution)/shard_map/swiglu_backward/pallas_call | solution.py:416
  88.6 2.5 %store.1 = (bf16[64,512]{1,0:T(8,128)(2,1)}, bf16[512,1792]{1,0:T(8,128)(2,1)}, bf16[512,1792]{1,0:T(8,128)(2,1)}, bf16[1792,512]{1,0:T(8,128)(2,1)}) custom-call(bf16[64,512]{1,0:T(8,128)(2,1)S(1)} %get-tuple-element.8.a, bf16[512,1792]{1,0:T(8,128)(2,1)S(1)} %get-tuple-element.9.b, bf16[512,1792]{1,0:T(8,128)(2,1)S(1)} %get-tuple-element.10.c, ...), custom_call_target="tpu_custom_call" | custom-call | tf_op jit(solution)/shard_map/store/pallas_call | solution.py:445

commit v4 on v3

--- a/solution.py
+++ b/solution.py
@@ -19,20 +19,19 @@
 PLANE = 256
 CHUNK = 128
 PART = 32
-ORDER = ((1, 0), (0, 0), (2, 1), (3, 0), (3, 1), (1, 1), (0, 1), (2, 0))
-DIRECT = ((1, 0), (0, 0), (2, 1), (3, 0), (3, 1), (1, 1))
+ORDER = ((3, 0), (0, 0), (2, 1), (1, 1), (2, 0), (0, 1), (1, 0), (3, 1))
+DIRECT = ((0, 0), (1, 1), (0, 1), (1, 0), (3, 1))
 N_COPY = 192
 SCHEDULE = (
-    ("g_x",), ("uz",), ("u_x",), ("turn_down",), ("turn_up",), ("gz0",), ("g_relay",), ("gz12",),
-    ("go_y",), ("s0", 1), ("s0", 6), ("u_other",), ("u_relay",), ("s0", 7), ("gz3",), ("s0", 0),
-    ("s0", 4), ("s1", 7), ("s1", 0), ("s0", 3), ("u_other_relay",), ("s0", 5), ("s1", 3), ("s0", 2),
-    ("s1", 5), ("s2", 7), ("s1", 4), ("s2", 0), ("gather_core",), ("tok_h",), ("s3", 7), ("s2", 3),
-    ("s1", 2), ("s3", 0), ("s2", 5), ("s1", 1), ("s2", 4), ("s4", 7), ("s1", 6), ("s2", 2),
-    ("tok_y",), ("s3", 3), ("s5", 0), ("s3", 5), ("core_arrive",), ("hidden",), ("s3", 2),
-    ("s3", 4), ("grad_down",), ("s5", 7), ("s2", 1), ("s2", 6), ("s6", 0), ("s5", 3), ("s6", 7),
-    ("s3", 1), ("s5", 5), ("s3", 6), ("s6", 3), ("s5", 2), ("s6", 5), ("s5", 4), ("s6", 2),
-    ("s5", 1), ("s6", 4), ("s4", 6), ("s6", 1), ("s7", 0), ("s5", 6), ("s6", 6), ("s7", 1), ("wg",),
-    ("final",),
+    ("u_x",), ("uz",), ("g_x",), ("turn_down",), ("turn_up",), ("u_relay",), ("tok_h",), ("go_y",),
+    ("s0", 1), ("s0", 5), ("g_relay",), ("gz12",), ("u_other",), ("s0", 2), ("s0", 3), ("gz3",),
+    ("s1", 2), ("s0", 0), ("s0", 4), ("s1", 0), ("s0", 6), ("s0", 7), ("s1", 4), ("s2", 2),
+    ("s1", 6), ("s2", 0), ("u_other_relay",), ("s1", 7), ("s2", 4), ("gz0",), ("s2", 6), ("s3", 2),
+    ("s3", 0), ("tok_y",), ("s3", 4), ("s2", 7), ("s1", 3), ("s4", 2), ("s1", 1), ("s4", 0),
+    ("s4", 4), ("gather_core",), ("s3", 6), ("s2", 3), ("s1", 5), ("s5", 2), ("s3", 7), ("s2", 1),
+    ("s5", 0), ("s3", 3), ("s5", 4), ("core_arrive",), ("s6", 2), ("s5", 6), ("s3", 1), ("s6", 0),
+    ("s2", 5), ("s6", 4), ("s5", 7), ("s6", 6), ("s5", 3), ("s3", 5), ("s6", 7), ("s5", 1),
+    ("s6", 3), ("s6", 1), ("s7", 0), ("s5", 5), ("s6", 5), ("s7", 1), ("wg",), ("final",),
 )
 
 
@@ -46,8 +45,8 @@
 
 def kernel(
     tok_in, gate_in, up_in, go_in, wg_in, wu_in, wd_in,
-    gt_out, gg_out, gu_out, gd_out,
-    wg, wu, wd, wg_t, wu_t, wd_t, tok, go, gate, up, hid, ggrad, ugrad, hg,
+    gt_out, gg_out, gu_out, hid, go_out,
+    wg, wu, wd, wg_t, wu_t, wd_t, tok, go, gate, up, ggrad, ugrad, hg,
     keep, sib_send, sib_recv, x_send, x_recv, acc, z_send, z_recv,
     d_send, d_recv, d_sum, h_send, h_recv,
     send_sem, recv_sem, local_sem,
@@ -210,6 +209,7 @@
                 ts = t * s
                 ggrad[p, o, c] = (ts * u * (1.0 + g * (1.0 - s))).astype(BF16)
                 ugrad[p, o, c] = (ts * g).astype(BF16)
+                hid[p, o, c] = (g * s * u).astype(BF16)
 
         o = rows(j, 0, CHUNK)
         part = dot(ggrad[p, o], wg_t[...], NN) + dot(ugrad[p, o], wu_t[...], NN)
@@ -235,20 +235,6 @@
             def _():
                 c.start()
 
-    def hidden():
-        @pl.loop(0, 64, unroll=4)
-        def _(i):
-            r = ds(i % 4 * 16, 16)
-            b = i // 4
-            o = ds(b % 4 * 64 + i % 4 * 16, 16)
-            g = gate[b // 2, b % 2, r].astype(F32)
-            u = up[b // 2, b % 2, r].astype(F32)
-            hid[b // 4, o] = (g * u * (1.0 / (1.0 + jnp.exp(-g)))).astype(BF16)
-
-    def grad_down():
-        a, b = hid[...].reshape(TOK, HID), go[...].reshape(TOK, FEAT)
-        gd_out[...] = dot(a, b, TN).astype(BF16)
-
     def tok_h():
         got["tok_h"] = [send(tok_in, tok.at[y, zh], dzh=d) for d in (2, 1, 3)]
 
@@ -320,12 +306,13 @@
         arrive(go_h)
         l_go.wait()
         got["go_y"] = {}
-        for d, h in ((2, 0), (3, 0), (1, 1), (1, 0), (3, 1), (2, 1)):
+        for d, h in ((2, 1), (3, 1), (2, 0), (1, 0), (1, 1), (3, 0)):
             q = go.at[y, 2 * h : 2 * h + 2]
             got["go_y"][d, h] = send(q, q, dy=d)
 
     def core_arrive():
         arrive(got["core"])
+        go_out[...] = go[...]
 
     def turn_down():
         l_wd.wait()
@@ -360,31 +347,29 @@
     l_wu = load(wu_in, wu)
 
     steps = dict(
+        u_x=u_x,
+        uz=uz,
         g_x=g_x,
-        uz=uz,
-        u_x=u_x,
         turn_down=turn_down,
         turn_up=turn_up,
-        gz0=gz0,
+        u_relay=u_relay,
+        tok_h=tok_h,
+        go_y=go_y,
+        s0=s0,
         g_relay=g_relay,
         gz12=gz12,
-        go_y=go_y,
-        s0=s0,
         u_other=u_other,
-        u_relay=u_relay,
         gz3=gz3,
         s1=s1,
+        s2=s2,
         u_other_relay=u_other_relay,
-        s2=s2,
+        gz0=gz0,
+        s3=s3,
+        tok_y=tok_y,
+        s4=s4,
         gather_core=gather_core,
-        tok_h=tok_h,
-        s3=s3,
-        s4=s4,
-        tok_y=tok_y,
         s5=s5,
         core_arrive=core_arrive,
-        hidden=hidden,
-        grad_down=grad_down,
         s6=s6,
         s7=s7,
         wg=wg_grads,
@@ -396,13 +381,23 @@
         c.wait_send()
 
 
-def store(a, b, c, d, a_out, b_out, c_out, d_out, sem):
-    moves = [
-        pltpu.make_async_copy(src, dst, sem.at[i])
-        for i, (src, dst) in enumerate(((b, b_out), (c, c_out), (d, d_out), (a, a_out)))
-    ]
-    for m in moves:
-        m.start()
+def finish(gt, gg, gu, hid, go, gt_out, gg_out, gu_out, gd_out, gd, sem):
+    moves = []
+
+    def move(src, dst):
+        moves.append(pltpu.make_async_copy(src, dst, sem.at[len(moves)]))
+        moves[-1].start()
+
+    for src, dst in ((gg, gg_out), (gu, gu_out)):
+        for i in range(2):
+            r = pl.ds(i * FEAT // 2, FEAT // 2)
+            move(src.at[r], dst.at[r])
+    move(gt, gt_out)
+    b = go[...].reshape(TOK, FEAT)
+    for i in range(7):
+        r = pl.ds(i * 256, 256)
+        gd[r] = dot(hid[:, :, r].reshape(TOK, 256), b, TN).astype(BF16)
+        move(gd.at[r], gd_out.at[r])
     for m in moves:
         m.wait()
 
@@ -415,15 +410,17 @@
     n = len(ORDER)
     made = pl.pallas_call(
         kernel,
-        out_shape=(bf(64, FEAT), bf(FEAT, HID), bf(FEAT, HID), bf(HID, FEAT)),
+        out_shape=(
+            bf(64, FEAT), bf(FEAT, HID), bf(FEAT, HID), bf(4, PLANE, HID), bf(4, 4, 64, FEAT)
+        ),
         in_specs=[hbm] * 7,
-        out_specs=(vmem,) * 4,
+        out_specs=(vmem,) * 5,
         scratch_shapes=[
             bf(FEAT, HID), bf(FEAT, HID), bf(HID, FEAT),
             bf(HID, FEAT), bf(HID, FEAT), bf(FEAT, HID),
             bf(4, 4, 64, FEAT), bf(4, 4, 64, FEAT),
             bf(8, 2, 64, HID), bf(8, 2, 64, HID),
-            bf(4, PLANE, HID), bf(4, PLANE, HID), bf(4, PLANE, HID),
+            bf(4, PLANE, HID), bf(4, PLANE, HID),
             bf(2, 4, PLANE, HALF),
             fl(n, CHUNK, HALF), fl(n, CHUNK, HALF), fl(n, CHUNK, HALF),
             bf(n, CHUNK, HALF), bf(n, 3, PART, HALF),
@@ -435,21 +432,24 @@
             pltpu.SemaphoreType.DMA((8,)),
         ],
         compiler_params=pltpu.CompilerParams(
-            collective_id=0, has_side_effects=True, vmem_limit_bytes=57 * 2**20
+            collective_id=0, has_side_effects=True, vmem_limit_bytes=53 * 2**20
         ),
         cost_estimate=pl.CostEstimate(
-            flops=12 * TOK * FEAT * HID, bytes_accessed=2**24, transcendentals=TOK * HID
+            flops=10 * TOK * FEAT * HID, bytes_accessed=2**24, transcendentals=TOK * HID
         ),
         name="swiglu_backward",
     )(tokens, gate_pre, up_pre, grad_out, gate_weight, up_weight, down_weight)
     return pl.pallas_call(
-        store,
-        out_shape=tuple(jax.ShapeDtypeStruct(m.shape, BF16) for m in made),
-        in_specs=[vmem] * 4,
+        finish,
+        out_shape=tuple(
+            jax.ShapeDtypeStruct(shape, BF16)
+            for shape in ((64, FEAT), (FEAT, HID), (FEAT, HID), (HID, FEAT))
+        ),
+        in_specs=[vmem] * 5,
         out_specs=(hbm,) * 4,
-        scratch_shapes=[pltpu.SemaphoreType.DMA((4,))],
-        compiler_params=pltpu.CompilerParams(vmem_limit_bytes=2**20),
-        name="store",
+        scratch_shapes=[bf(HID, FEAT), pltpu.SemaphoreType.DMA((12,))],
+        compiler_params=pltpu.CompilerParams(vmem_limit_bytes=10 * 2**20),
+        name="finish",
     )(*(pltpu.with_memory_space_constraint(m, pltpu.VMEM) for m in made))
 
 

time: 91.3 us -> 89.1 us (0.976)
  Pallas kernels: 90.4 us -> 87.5 us
    pallas_call x1, Pallas kernels: 87.9 us -> 84.6 us  [on_device(): pl.pallas_call(kernel, out_shape=(bf(64, FEAT), bf(FEAT, HID), bf(FEAT, H...]
where the time goes in v4:
time: 89.1 us; the launch traced here: 88.3 us
  Pallas kernels  87.5 us (98%)
    pallas_call x1, Pallas kernels, on_device(): pl.pallas_call(kernel, out_shape=(bf(64, FEAT), bf(FEAT, HID), bf(FEAT, H...  84.6 us
    pallas_call x1, Pallas kernels, on_device(): pl.pallas_call(finish, out_shape=tuple((jax.ShapeDtypeStruct(shape, BF16)...  2.9 us

profile of v4, /device:TPU:1, one launch (start us, length us, event | category | flops | bytes accessed | tf_op | source)
XLA Modules:
  0.0 88.3 jit_solution(9251853876644985991)
XLA Ops:
  0.6 84.6 %swiglu_backward.1 = (bf16[64,512]{1,0:T(8,128)(2,1)S(1)}, bf16[512,1792]{1,0:T(8,128)(2,1)S(1)}, bf16[512,1792]{1,0:T(8,128)(2,1)S(1)}, bf16[4,256,1792]{2,1,0:T(8,128)(2,1)S(1)}, bf16[4,4,64,512]{3,2,1,0:T(8,128)(2,1)S(1)}) custom-call(bf16[64,512]{1,0:T(8,128)(2,1)} %tok_in.1, bf16[64,1792]{1,0:T(8,128)(2,1)} %gate_in.1, bf16[64,1792]{1,0:T(8,128)(2,1)} %up_in.1, ...), custom_call_target="tpu_custom_call" | custom-call | flops 9395240960 | bytes 16777216 | tf_op jit(solution)/shard_map/swiglu_backward/pallas_call | solution.py:411
  85.2 2.9 %finish.1 = (bf16[64,512]{1,0:T(8,128)(2,1)}, bf16[512,1792]{1,0:T(8,128)(2,1)}, bf16[512,1792]{1,0:T(8,128)(2,1)}, bf16[1792,512]{1,0:T(8,128)(2,1)}) custom-call(bf16[64,512]{1,0:T(8,128)(2,1)S(1)} %get-tuple-element.9.gt, bf16[512,1792]{1,0:T(8,128)(2,1)S(1)} %get-tuple-element.10.gg, bf16[512,1792]{1,0:T(8,128)(2,1)S(1)} %get-tuple-element.11.gu, ...), custom_call_target="tpu_custom_call" | custom-call | tf_op jit(solution)/shard_map/finish/pallas_call | solution.py:442

commit v5 on v4

--- a/solution.py
+++ b/solution.py
@@ -141,7 +141,7 @@
     def s1(j):
         st[j]["sib"].wait_recv()
 
-        @pl.loop(0, CHUNK // 16)
+        @pl.loop(0, CHUNK // 16, unroll=True)
         def _(i):
             r = ds(i * 16, 16)
             x_send[j, r] = (keep[j, r] + sib_recv[j, r]).astype(BF16)
@@ -196,7 +196,7 @@
         dy, half = ORDER[j]
         for b in range(2):
 
-            @pl.loop(0, 8, unroll=4)
+            @pl.loop(0, 8, unroll=True)
             def _(i):
                 r = ds(i // 2 * 16, 16)
                 o = rows(j, b * 64 + i // 2 * 16, 16)

time: 89.1 us -> 88.6 us (level)
  no operation moved by 1% of the time
where the time goes in v5:
time: 88.6 us
  Pallas kernels  87.8 us (99%)
    pallas_call x1, Pallas kernels, on_device(): pl.pallas_call(kernel, out_shape=(bf(64, FEAT), bf(FEAT, HID), bf(FEAT, H...  84.9 us
    pallas_call x1, Pallas kernels, on_device(): pl.pallas_call(finish, out_shape=tuple((jax.ShapeDtypeStruct(shape, BF16)...  2.9 us

profile of v5, /device:TPU:1, one launch (start us, length us, event | category | flops | bytes accessed | tf_op | source)
XLA Modules:
  0.0 88.6 jit_solution(15018003460335316663)
XLA Ops:
  0.6 84.9 %swiglu_backward.1 = (bf16[64,512]{1,0:T(8,128)(2,1)S(1)}, bf16[512,1792]{1,0:T(8,128)(2,1)S(1)}, bf16[512,1792]{1,0:T(8,128)(2,1)S(1)}, bf16[4,256,1792]{2,1,0:T(8,128)(2,1)S(1)}, bf16[4,4,64,512]{3,2,1,0:T(8,128)(2,1)S(1)}) custom-call(bf16[64,512]{1,0:T(8,128)(2,1)} %tok_in.1, bf16[64,1792]{1,0:T(8,128)(2,1)} %gate_in.1, bf16[64,1792]{1,0:T(8,128)(2,1)} %up_in.1, ...), custom_call_target="tpu_custom_call" | custom-call | flops 9395240960 | bytes 16777216 | tf_op jit(solution)/shard_map/swiglu_backward/pallas_call | solution.py:411
  85.5 2.9 %finish.1 = (bf16[64,512]{1,0:T(8,128)(2,1)}, bf16[512,1792]{1,0:T(8,128)(2,1)}, bf16[512,1792]{1,0:T(8,128)(2,1)}, bf16[1792,512]{1,0:T(8,128)(2,1)}) custom-call(bf16[64,512]{1,0:T(8,128)(2,1)S(1)} %get-tuple-element.9.gt, bf16[512,1792]{1,0:T(8,128)(2,1)S(1)} %get-tuple-element.10.gg, bf16[512,1792]{1,0:T(8,128)(2,1)S(1)} %get-tuple-element.11.gu, ...), custom_call_target="tpu_custom_call" | custom-call | tf_op jit(solution)/shard_map/finish/pallas_call | solution.py:442
